TPU v7x, 32 devices: a whole 2x2x4 slice. The times are simulated.
32 devices in a mesh: groups: 2 (over x), ctx: 8 (over z, y), dp: 2 (over core).
Axes of the slice: x: 2, y: 2, z: 4, core: 2. Of those that a mesh axis runs over, the one named last changes fastest.
Arguments:
- inputs: bfloat16 [4, 4096, 256], P(('groups', 'dp'), 'ctx'), parts along dimension 0, may hold values from -6 to 6
- value_weight: bfloat16 [256, 256], replicated, may hold values from -0.375 to 0.375
- gate_weight: bfloat16 [256, 256], replicated, may hold values from -0.375 to 0.375
- output_weight: bfloat16 [256, 256], replicated, may hold values from -0.375 to 0.375
- filters: bfloat16 [4096, 256], P('ctx'), may hold values from -0.09375 to 0.09375
- cotangent: bfloat16 [4, 4096, 256], P(('groups', 'dp'), 'ctx'), parts along dimension 0, may hold values from -6 to 6
Outputs:
- input_grad: bfloat16 [4, 4096, 256], P(('groups', 'dp'), 'ctx'), parts along dimension 0
- proj_grads: float32 [6, 256, 256], P('groups', 'ctx'), parts along dimension 0
- filter_grads: float32 [8192, 256], P(('groups', 'ctx')), parts along dimension 0
There are 2 independent parts, one for each index of `groups`. A program takes and returns all parts, laid end to end along the dimension named above; an argument that names none is the same for every part. Nothing has to cross between parts.
All inputs are finite; a program needn't handle non-finite values.
Results may differ from a plain program's by a relative error of at most 0.0057.
Values may be sent and summed in bfloat16 or wider, within the bound.
A program may use at most 64 MiB of HBM per device.

v0:
```python
import math
import jax
import jax.numpy as jnp
from jax import lax
from jax.sharding import PartitionSpec as P


def phase_table(left, right, modulus, sign):
    product = left[:, None] * right[None, :] % modulus
    return sign * (2.0 * math.pi / modulus) * product.astype(jnp.float32)


def dft_matrix(size, sign):
    counter = jnp.arange(size, dtype=jnp.int32)
    phase = phase_table(counter, counter, size, sign)
    return (jnp.cos(phase), jnp.sin(phase))


def apply_left(matrix, field):
    return jnp.tensordot(matrix, field, axes=(1, 0), precision=lax.Precision.HIGHEST)


def mix_first(cos_table, sin_table, real_part, imag_part):
    new_real = apply_left(cos_table, real_part) - apply_left(sin_table, imag_part)
    new_imag = apply_left(cos_table, imag_part) + apply_left(sin_table, real_part)
    return (new_real, new_imag)


def apply_middle(matrix, field):
    return jnp.einsum("kb,abw->akw", matrix, field, precision=lax.Precision.HIGHEST)


def mix_second(cos_table, sin_table, real_part, imag_part):
    new_real = apply_middle(cos_table, real_part) - apply_middle(sin_table, imag_part)
    new_imag = apply_middle(cos_table, imag_part) + apply_middle(sin_table, real_part)
    return (new_real, new_imag)


def rotate(real_part, imag_part, cos_part, sin_part):
    return (
        real_part * cos_part - imag_part * sin_part,
        real_part * sin_part + imag_part * cos_part,
    )


def local_dft(real_part, imag_part, sign):
    length = real_part.shape[0]
    columns = real_part.shape[1]
    outer = 32
    inner = length // outer
    real_part = real_part.reshape(outer, inner, columns)
    imag_part = imag_part.reshape(outer, inner, columns)
    cos_table, sin_table = dft_matrix(outer, sign)
    real_part, imag_part = mix_first(cos_table, sin_table, real_part, imag_part)
    phase = phase_table(
        jnp.arange(outer, dtype=jnp.int32), jnp.arange(inner, dtype=jnp.int32), length, sign
    )[:, :, None]
    real_part, imag_part = rotate(real_part, imag_part, jnp.cos(phase), jnp.sin(phase))
    cos_table, sin_table = dft_matrix(inner, sign)
    real_part, imag_part = mix_second(cos_table, sin_table, real_part, imag_part)
    real_part = real_part.transpose(1, 0, 2).reshape(length, columns)
    imag_part = imag_part.transpose(1, 0, 2).reshape(length, columns)
    return (real_part, imag_part)


def forward_transform(stacked):
    count = lax.axis_size("ctx")
    place = lax.axis_index("ctx")
    tok_rows = stacked.shape[0]
    total = count * tok_rows
    piece = tok_rows // count
    moved = lax.all_to_all(stacked[None], "ctx", split_axis=1, concat_axis=0, tiled=True)
    real_rows = moved.astype(jnp.float32)
    cos_table, sin_table = dft_matrix(count, -1.0)
    real_part = apply_left(cos_table, real_rows)
    imag_part = apply_left(sin_table, real_rows)
    row_index = place * piece + jnp.arange(piece, dtype=jnp.int32)
    phase = phase_table(jnp.arange(count, dtype=jnp.int32), row_index, total, -1.0)[:, :, None]
    real_part, imag_part = rotate(real_part, imag_part, jnp.cos(phase), jnp.sin(phase))
    real_part, imag_part = (
        lax.all_to_all(real_part, "ctx", split_axis=0, concat_axis=1, tiled=True),
        lax.all_to_all(imag_part, "ctx", split_axis=0, concat_axis=1, tiled=True),
    )
    return local_dft(real_part[0], imag_part[0], -1.0)


def inverse_transform(real_part, imag_part):
    count = lax.axis_size("ctx")
    place = lax.axis_index("ctx")
    tok_rows = real_part.shape[0]
    total = count * tok_rows
    real_part, imag_part = local_dft(real_part, imag_part, 1.0)
    product = place * jnp.arange(tok_rows, dtype=jnp.int32) % total
    phase = (2.0 * math.pi / total * product.astype(jnp.float32))[:, None]
    real_part, imag_part = rotate(real_part, imag_part, jnp.cos(phase), jnp.sin(phase))
    real_part, imag_part = (
        lax.all_to_all(real_part[None], "ctx", split_axis=1, concat_axis=0, tiled=True),
        lax.all_to_all(imag_part[None], "ctx", split_axis=1, concat_axis=0, tiled=True),
    )
    cos_table, sin_table = dft_matrix(count, 1.0)
    rows_part = apply_left(cos_table, real_part) - apply_left(sin_table, imag_part)
    returned = lax.all_to_all(rows_part, "ctx", split_axis=0, concat_axis=1, tiled=True)
    return returned[0] * (1.0 / total)


def contract_rows(left_rows, right_rows):
    return lax.dot_general(
        left_rows, right_rows, (((0,), (0,)), ((), ())), preferred_element_type=jnp.float32
    )


def times_transpose(left_rows, weight):
    return lax.dot_general(
        left_rows, weight, (((1,), (1,)), ((), ())), preferred_element_type=jnp.float32
    )


def local(inputs, value_weight, gate_weight, output_weight, filters, cotangent):
    token_rows = inputs[0]
    upstream = cotangent[0]
    tok_rows = token_rows.shape[0]
    width = token_rows.shape[1]
    value_act = jnp.dot(token_rows, value_weight, preferred_element_type=jnp.float32).astype(
        jnp.bfloat16
    )
    gate_act = jnp.dot(token_rows, gate_weight, preferred_element_type=jnp.float32)
    d_gated = times_transpose(upstream, output_weight)
    d_mixed = (d_gated * gate_act).astype(jnp.bfloat16)
    share = width // lax.axis_size("dp")
    kernel_part = lax.dynamic_slice_in_dim(filters, lax.axis_index("dp") * share, share, 1)
    spec_real, spec_imag = forward_transform(
        jnp.concatenate([value_act, d_mixed, kernel_part], axis=1)
    )
    value_real = spec_real[:, :width]
    value_imag = spec_imag[:, :width]
    grad_real = spec_real[:, width : 2 * width]
    grad_imag = spec_imag[:, width : 2 * width]
    kernel_real = spec_real[:, 2 * width :]
    kernel_imag = spec_imag[:, 2 * width :]
    kernel_real, kernel_imag = (
        lax.all_gather(kernel_real, "dp", axis=1, tiled=True),
        lax.all_gather(kernel_imag, "dp", axis=1, tiled=True),
    )
    mixed_real = value_real * kernel_real - value_imag * kernel_imag
    mixed_imag = value_real * kernel_imag + value_imag * kernel_real
    back_real = grad_real * kernel_real + grad_imag * kernel_imag
    back_imag = grad_imag * kernel_real - grad_real * kernel_imag
    corr_real = grad_real * value_real + grad_imag * value_imag
    corr_imag = grad_imag * value_real - grad_real * value_imag
    grad_scale = 1.0 / math.sqrt(lax.axis_size("dp") * lax.axis_size("ctx") * tok_rows)
    rows_all = inverse_transform(
        jnp.concatenate([mixed_real, back_real, corr_real], axis=1),
        jnp.concatenate([mixed_imag, back_imag, corr_imag], axis=1),
    )
    mixed_act = rows_all[:, :width]
    d_value = rows_all[:, width : 2 * width].astype(jnp.bfloat16)
    filter_terms = rows_all[:, 2 * width :] * grad_scale
    gated = (gate_act * mixed_act).astype(jnp.bfloat16)
    d_gate = (d_gated * mixed_act).astype(jnp.bfloat16)
    input_rows = times_transpose(d_value, value_weight) + times_transpose(d_gate, gate_weight)
    input_grad = input_rows.astype(jnp.bfloat16)[None]
    proj_terms = (
        jnp.stack(
            [
                contract_rows(token_rows, d_value),
                contract_rows(token_rows, d_gate),
                contract_rows(gated, upstream),
            ],
            axis=0,
        )
        * grad_scale
    )
    proj_part = lax.psum_scatter(proj_terms, "ctx", scatter_dimension=1, tiled=True)
    proj_grads, filter_grads = lax.psum((proj_part, filter_terms), "dp")
    return (input_grad, proj_grads, filter_grads)


def solution(mesh):
    return jax.shard_map(
        local,
        mesh=mesh,
        in_specs=(
            P(("groups", "dp"), "ctx", None),
            P(),
            P(),
            P(),
            P("ctx", None),
            P(("groups", "dp"), "ctx", None),
        ),
        out_specs=(
            P(("groups", "dp"), "ctx", None),
            P("groups", "ctx", None),
            P(("groups", "ctx"), None),
        ),
        check_vma=False,
    )
```

profile of v0, /device:TPU:0, one launch (start us, length us, event | category | flops | bytes accessed | tf_op | source)
XLA Modules:
  0.0 413.0 jit_solution(4538042132011072606)
XLA Ops:
  13.6 4.6 %reduce = bf16[512,640]{1,0:T(8,128)(2,1)S(1)} reduce(bf16[512,1,640]{2,1,0:T(2,128)(2,1)S(1)} %bitcast.141, bf16[]{:T(256)} %broadcast.401), dimensions={1}, to_apply=%bitcast.105.reduce_sub_computation | reduce | bytes 1310722
  19.3 7.3 %all-to-all-start = ((bf16[8,2,20480]{2,1,0:T(2,128)(2,1)}), bf16[8,2,20480]{2,1,0:T(2,128)(2,1)S(1)}, u32[]{:S(2)}, u32[]{:S(2)}) async-start(bf16[8,2,20480]{2,1,0:T(2,128)(2,1)} %reshape.329), calls=%async_computation | async-start | bytes 1310720 | tf_op jit(solution)/shard_map/all_to_all | solution.py:72
  26.8 17.1 %all-to-all-done = bf16[8,2,20480]{2,1,0:T(2,128)(2,1)S(1)} async-done(((bf16[8,2,20480]{2,1,0:T(2,128)(2,1)}), bf16[8,2,20480]{2,1,0:T(2,128)(2,1)S(1)}, u32[]{:S(2)}, u32[]{:S(2)}) %all-to-all-start) | async-done | bytes 655392 | tf_op jit(solution)/shard_map/all_to_all | solution.py:72
  47.9 3.6 all-to-all-start.1
  52.9 30.2 %all-to-all-done.1 = f32[8,64,640]{2,1,0:T(8,128)S(1)} async-done(((f32[8,64,640]{2,1,0:T(8,128)}), f32[8,64,640]{2,1,0:T(8,128)S(1)}, u32[]{:S(2)}, u32[]{:S(2)}) %all-to-all-start.1) | async-done | bytes 1310752 | tf_op jit(solution)/shard_map/all_to_all | solution.py:81
  83.1 3.9 all-to-all-start.2
  87.3 2.6 fusion.31
  89.9 28.5 %all-to-all-done.2 = f32[8,64,640]{2,1,0:T(8,128)S(1)} async-done(((f32[8,64,640]{2,1,0:T(8,128)}), f32[8,64,640]{2,1,0:T(8,128)S(1)}, u32[]{:S(2)}, u32[]{:S(2)}) %all-to-all-start.2) | async-done | bytes 1310752 | tf_op jit(solution)/shard_map/all_to_all | solution.py:82
  127.1 12.8 %convolution_subtract_fusion.2 = f32[16,32,640]{2,0,1:T(8,128)S(1)} fusion(f32[16,32,640]{2,0,1:T(8,128)S(1)} %fusion.25, f32[32,16,640]{2,0,1:T(8,128)S(1)} %get-tuple-element.28), kind=kOutput, calls=%fused_computation.32 | convolution fusion | flops 63245824 | bytes 3932160 | tf_op jit(solution)/shard_map/kb,abw->akw/dot_general | solution.py:30
  147.5 2.3 fusion.19
  149.9 2.3 fusion.15
  152.3 2.4 convolution_subtract_fusion.1
  154.6 2.7 multiply_subtract_fusion
  157.3 2.4 fusion.13
  165.1 2.2 convolution_add_fusion
  168.6 2.8 copy.121
  171.4 4.1 all-to-all-start.4
  175.5 2.8 copy.119
  178.3 34.6 %all-to-all-done.4 = f32[1,512,768]{2,0,1:T(1,128)S(1)} async-done(((f32[1,512,768]{2,0,1:T(1,128)}), f32[1,512,768]{2,0,1:T(1,128)S(1)}, u32[]{:S(2)}, u32[]{:S(2)}) %all-to-all-start.4) | async-done | bytes 1572896 | tf_op jit(solution)/shard_map/all_to_all | solution.py:98
  212.9 3.6 all-to-all-start.3
  218.9 34.8 %all-to-all-done.3 = f32[1,512,768]{2,0,1:T(1,128)S(1)} async-done(((f32[1,512,768]{2,0,1:T(1,128)}), f32[1,512,768]{2,0,1:T(1,128)S(1)}, u32[]{:S(2)}, u32[]{:S(2)}) %all-to-all-start.3) | async-done | bytes 1572896 | tf_op jit(solution)/shard_map/all_to_all | solution.py:97
  256.5 40.6 %all_to_all.63 = f32[8,64,768]{2,1,0:T(8,128)S(1)} all-to-all(f32[8,64,768]{2,1,0:T(8,128)S(1)} %copy.123), channel_id=1, replica_groups=mesh['groups'=2,'ctx'=8,'dp'=2] {'ctx'}, dimensions={0} | all-to-all | bytes 3145728 | tf_op jit(solution)/shard_map/all_to_all | solution.py:102
  305.0 75.9 %all-reduce.5.cloned.1.call-done = f32[3,256,256]{2,0,1:T(4,128)} async-done(((f32[3,256,256]{2,0,1:T(4,128)}), f32[3,256,256]{2,0,1:T(4,128)}) %all-reduce.5.cloned.1.call-update) | async-done | bytes 786448
  383.7 18.9 %all-reduce.7.cloned.1.call-done = (f32[3,32,256]{2,0,1:T(4,128)}, f32[512,256]{1,0:T(8,128)}) async-done(((f32[3,32,256]{2,0,1:T(4,128)}, f32[512,256]{1,0:T(8,128)}), (f32[3,32,256]{2,0,1:T(4,128)}, f32[512,256]{1,0:T(8,128)})) %all-reduce.7.cloned.1.call-update) | async-done | bytes 622608 | tf_op jit(solution)/shard_map/psum | solution.py:174
  (88 shorter events, 54.6 us)
Async XLA Ops:
  7.2 1.1 copy-start
  7.2 3.7 copy-start.5
  7.2 3.7 copy-start.9
  9.5 1.3 copy-start.2
  19.3 24.6 %all-to-all-start = ((bf16[8,2,20480]{2,1,0:T(2,128)(2,1)}), bf16[8,2,20480]{2,1,0:T(2,128)(2,1)S(1)}, u32[]{:S(2)}, u32[]{:S(2)}) async-start(bf16[8,2,20480]{2,1,0:T(2,128)(2,1)} %reshape.329), calls=%async_computation | async-start | bytes 1310720 | tf_op jit(solution)/shard_map/all_to_all | solution.py:72
  47.9 35.2 %all-to-all-start.1 = ((f32[8,64,640]{2,1,0:T(8,128)}), f32[8,64,640]{2,1,0:T(8,128)S(1)}, u32[]{:S(2)}, u32[]{:S(2)}) async-start(f32[8,64,640]{2,1,0:T(8,128)} %copy.97), calls=%async_computation.1 | async-start | bytes 2621440 | tf_op jit(solution)/shard_map/all_to_all | solution.py:81
  83.1 35.2 %all-to-all-start.2 = ((f32[8,64,640]{2,1,0:T(8,128)}), f32[8,64,640]{2,1,0:T(8,128)S(1)}, u32[]{:S(2)}, u32[]{:S(2)}) async-start(f32[8,64,640]{2,1,0:T(8,128)} %copy.99), calls=%async_computation.2 | async-start | bytes 2621440 | tf_op jit(solution)/shard_map/all_to_all | solution.py:82
  118.3 1.6 copy-start.1
  171.4 41.5 %all-to-all-start.4 = ((f32[1,512,768]{2,0,1:T(1,128)}), f32[1,512,768]{2,0,1:T(1,128)S(1)}, u32[]{:S(2)}, u32[]{:S(2)}) async-start(f32[1,512,768]{2,0,1:T(1,128)} %copy.121), calls=%async_computation.4 | async-start | bytes 3145728 | tf_op jit(solution)/shard_map/all_to_all | solution.py:98
  212.9 40.8 %all-to-all-start.3 = ((f32[1,512,768]{2,0,1:T(1,128)}), f32[1,512,768]{2,0,1:T(1,128)S(1)}, u32[]{:S(2)}, u32[]{:S(2)}) async-start(f32[1,512,768]{2,0,1:T(1,128)} %copy.119), calls=%async_computation.3 | async-start | bytes 3145728 | tf_op jit(solution)/shard_map/all_to_all | solution.py:97
  216.5 164.3 %all-reduce.5.cloned.1.call-start = ((), (), s32[]{:S(2)}) async-start(), calls=%async_computation.6 | async-start | bytes 2097152
  298.3 2.3 copy-start.3
  299.3 2.6 copy-start.4
  300.6 1.6 copy-start.6
  302.3 1.4 copy-start.10
  302.3 80.1 %copy-start.7 = (bf16[256,256]{1,0:T(8,128)(2,1)S(1)}, bf16[256,256]{1,0:T(8,128)(2,1)}, u32[]{:S(2)}) copy-start(bf16[256,256]{1,0:T(8,128)(2,1)} %param.7) | copy-start | bytes 393220
  303.6 79.1 %copy-start.8 = (bf16[256,256]{1,0:T(8,128)(2,1)S(1)}, bf16[256,256]{1,0:T(8,128)(2,1)}, u32[]{:S(2)}) copy-start(bf16[256,256]{1,0:T(8,128)(2,1)} %param.8) | copy-start | bytes 393220
  303.7 98.9 %all-reduce.7.cloned.1.call-start = ((), (), s32[]{:S(2)}) async-start(), calls=%async_computation.7 | async-start | bytes 1310720 | tf_op jit(solution)/shard_map/psum | solution.py:174
Sparse Core Ops, SparseCore 0:
  303.8 77.0 all-reduce.4
  383.9 18.5 all-reduce.6
where the time goes:
time: 420 us; the launch traced here: 413 us
  waiting for transfers between devices  240 us (57%)
  matrix products  58.3 us (14%)
  blocking collectives  44.9 us (11%)
  local copies, waits for them, and re-layouts  24.5 us (6%)
  starting transfers between devices  22.6 us (5%)
  between operations  15.4 us (4%)
  other arithmetic  7.2 us (2%)
    unnamed x3, waiting for transfers between devices  75.9 us
    all_to_all x1, blocking collectives, inverse_transform(): lax.all_to_all(rows_part, 'ctx', split_axis=0, concat_axis=1, tiled=True)  40.6 us
    all_to_all x1, waiting for transfers between devices, inverse_transform(): lax.all_to_all(real_part[None], 'ctx', split_axis=1, concat_axis=0, tiled...  34.8 us
    all_to_all x1, waiting for transfers between devices, inverse_transform(): lax.all_to_all(imag_part[None], 'ctx', split_axis=1, concat_axis=0, tiled...  34.6 us
    all_to_all x1, waiting for transfers between devices, forward_transform(): lax.all_to_all(real_part, 'ctx', split_axis=0, concat_axis=1, tiled=True)  30.2 us
    all_to_all x1, waiting for transfers between devices, forward_transform(): lax.all_to_all(imag_part, 'ctx', split_axis=0, concat_axis=1, tiled=True)  28.5 us
    dot_general x8, matrix products, apply_middle(): jnp.einsum('kb,abw->akw', matrix, field, precision=lax.Precision.HIGHEST)  27.4 us
    dot_general x12, matrix products, apply_left(): jnp.tensordot(matrix, field, axes=(1, 0), precision=lax.Precision.HIGHEST)  23.7 us
  transfers between devices with their start and end apart: 7, of which 7 were waited for; matrix products, arithmetic and copies ran while one was open for 3% of the time, Pallas kernels for 0%

commit v1 on v0

--- a/solution.py
+++ b/solution.py
@@ -95,7 +95,12 @@
     real_part, imag_part = rotate(real_part, imag_part, jnp.cos(phase), jnp.sin(phase))
     real_part, imag_part = (
         lax.all_to_all(real_part[None], "ctx", split_axis=1, concat_axis=0, tiled=True),
-        lax.all_to_all(imag_part[None], "ctx", split_axis=1, concat_axis=0, tiled=True),
+        jnp.concatenate(
+            lax.all_to_all(
+                jnp.stack(jnp.split(imag_part[None], lax.axis_size("ctx"), axis=1)), "ctx", 0, 0
+            ),
+            axis=0,
+        ),
     )
     cos_table, sin_table = dft_matrix(count, 1.0)
     rows_part = apply_left(cos_table, real_part) - apply_left(sin_table, imag_part)

time: 420 us -> 423 us (level)
    unnamed x34 -> x42, local copies, waits for them, and re-layouts: 9.51 us -> 14.3 us
where the time goes in v1:
time: 423 us; the launch traced here: 416 us
  waiting for transfers between devices  239 us (57%)
  matrix products  59.5 us (14%)
  blocking collectives  44.9 us (11%)
  local copies, waits for them, and re-layouts  27.2 us (6%)
  starting transfers between devices  22.4 us (5%)
  between operations  15.7 us (4%)
  other arithmetic  7.19 us (2%)
    unnamed x3, waiting for transfers between devices  75.9 us
    all_to_all x1, blocking collectives, inverse_transform(): lax.all_to_all(rows_part, 'ctx', split_axis=0, concat_axis=1, tiled=True)  40.6 us
    all_to_all x1, waiting for transfers between devices, inverse_transform(): lax.all_to_all(jnp.stack(jnp.split(imag_part[None], lax.axis_size('ctx'),...  34.6 us
    all_to_all x1, waiting for transfers between devices, inverse_transform(): lax.all_to_all(real_part[None], 'ctx', split_axis=1, concat_axis=0, tiled...  33.6 us
    all_to_all x1, waiting for transfers between devices, forward_transform(): lax.all_to_all(real_part, 'ctx', split_axis=0, concat_axis=1, tiled=True)  30.3 us
    all_to_all x1, waiting for transfers between devices, forward_transform(): lax.all_to_all(imag_part, 'ctx', split_axis=0, concat_axis=1, tiled=True)  28.5 us
    dot_general x8, matrix products, apply_middle(): jnp.einsum('kb,abw->akw', matrix, field, precision=lax.Precision.HIGHEST)  27.4 us
    dot_general x12, matrix products, apply_left(): jnp.tensordot(matrix, field, axes=(1, 0), precision=lax.Precision.HIGHEST)  24.8 us
  transfers between devices with their start and end apart: 7, of which 7 were waited for; matrix products, arithmetic and copies ran while one was open for 3% of the time, Pallas kernels for 0%

profile of v1, /device:TPU:0, one launch (start us, length us, event | category | flops | bytes accessed | tf_op | source)
XLA Modules:
  0.0 415.7 jit_solution(12246677001142174243)
XLA Ops:
  13.6 4.6 %reduce = bf16[512,640]{1,0:T(8,128)(2,1)S(1)} reduce(bf16[512,1,640]{2,1,0:T(2,128)(2,1)S(1)} %bitcast.174, bf16[]{:T(256)} %broadcast.401), dimensions={1}, to_apply=%bitcast.139.reduce_sub_computation | reduce | bytes 1310722
  19.3 7.3 %all-to-all-start = ((bf16[8,2,20480]{2,1,0:T(2,128)(2,1)}), bf16[8,2,20480]{2,1,0:T(2,128)(2,1)S(1)}, u32[]{:S(2)}, u32[]{:S(2)}) async-start(bf16[8,2,20480]{2,1,0:T(2,128)(2,1)} %reshape.330), calls=%async_computation | async-start | bytes 1310720 | tf_op jit(solution)/shard_map/all_to_all | solution.py:72
  26.8 17.1 %all-to-all-done = bf16[8,2,20480]{2,1,0:T(2,128)(2,1)S(1)} async-done(((bf16[8,2,20480]{2,1,0:T(2,128)(2,1)}), bf16[8,2,20480]{2,1,0:T(2,128)(2,1)S(1)}, u32[]{:S(2)}, u32[]{:S(2)}) %all-to-all-start) | async-done | bytes 655392 | tf_op jit(solution)/shard_map/all_to_all | solution.py:72
  48.0 3.6 all-to-all-start.1
  52.9 30.3 %all-to-all-done.1 = f32[8,64,640]{2,1,0:T(8,128)S(1)} async-done(((f32[8,64,640]{2,1,0:T(8,128)}), f32[8,64,640]{2,1,0:T(8,128)S(1)}, u32[]{:S(2)}, u32[]{:S(2)}) %all-to-all-start.1) | async-done | bytes 1310752 | tf_op jit(solution)/shard_map/all_to_all | solution.py:81
  83.2 3.9 all-to-all-start.2
  87.2 2.6 fusion.32
  89.8 28.5 %all-to-all-done.2 = f32[8,64,640]{2,1,0:T(8,128)S(1)} async-done(((f32[8,64,640]{2,1,0:T(8,128)}), f32[8,64,640]{2,1,0:T(8,128)S(1)}, u32[]{:S(2)}, u32[]{:S(2)}) %all-to-all-start.2) | async-done | bytes 1310752 | tf_op jit(solution)/shard_map/all_to_all | solution.py:82
  127.1 12.7 %convolution_subtract_fusion.2 = f32[16,32,640]{2,0,1:T(8,128)S(1)} fusion(f32[16,32,640]{2,0,1:T(8,128)S(1)} %fusion.26, f32[32,16,640]{2,0,1:T(8,128)S(1)} %get-tuple-element.31), kind=kOutput, calls=%fused_computation.33 | convolution fusion | flops 63245824 | bytes 3932160 | tf_op jit(solution)/shard_map/kb,abw->akw/dot_general | solution.py:30
  147.5 2.3 fusion.20
  149.9 2.3 fusion.16
  152.2 2.4 convolution_subtract_fusion.1
  154.6 2.7 multiply_subtract_fusion
  157.3 2.4 fusion.14
  165.1 2.3 convolution_add_fusion
  174.2 3.6 all-to-all-start.4
  177.9 2.8 copy.154
  180.7 34.6 %all-to-all-done.4 = f32[8,1,64,768]{3,2,1,0:T(8,128)S(1)} async-done(((f32[8,1,64,768]{3,2,1,0:T(8,128)}), f32[8,1,64,768]{3,2,1,0:T(8,128)S(1)}, u32[]{:S(2)}, u32[]{:S(2)}) %all-to-all-start.4) | async-done | bytes 1572896 | tf_op jit(solution)/shard_map/all_to_all | solution.py:99
  215.3 3.6 all-to-all-start.3
  219.2 3.3 fusion
  222.6 33.6 %all-to-all-done.3 = f32[1,512,768]{2,0,1:T(1,128)S(1)} async-done(((f32[1,512,768]{2,0,1:T(1,128)}), f32[1,512,768]{2,0,1:T(1,128)S(1)}, u32[]{:S(2)}, u32[]{:S(2)}) %all-to-all-start.3) | async-done | bytes 1572896 | tf_op jit(solution)/shard_map/all_to_all | solution.py:97
  258.9 40.6 %all_to_all.56 = f32[8,64,768]{2,1,0:T(8,128)S(1)} all-to-all(f32[8,64,768]{2,1,0:T(8,128)S(1)} %copy.157), channel_id=1, replica_groups=mesh['groups'=2,'ctx'=8,'dp'=2] {'ctx'}, dimensions={0} | all-to-all | bytes 3145728 | tf_op jit(solution)/shard_map/all_to_all | solution.py:107
  307.4 75.9 %all-reduce.5.cloned.1.call-done = f32[3,256,256]{2,0,1:T(4,128)} async-done(((f32[3,256,256]{2,0,1:T(4,128)}), f32[3,256,256]{2,0,1:T(4,128)}) %all-reduce.5.cloned.1.call-update) | async-done | bytes 786448
  386.1 18.8 %all-reduce.7.cloned.1.call-done = (f32[3,32,256]{2,0,1:T(4,128)}, f32[512,256]{1,0:T(8,128)}) async-done(((f32[3,32,256]{2,0,1:T(4,128)}, f32[512,256]{1,0:T(8,128)}), (f32[3,32,256]{2,0,1:T(4,128)}, f32[512,256]{1,0:T(8,128)})) %all-reduce.7.cloned.1.call-update) | async-done | bytes 622608 | tf_op jit(solution)/shard_map/psum | solution.py:179
  (96 shorter events, 58.2 us)
Async XLA Ops:
  7.2 1.1 copy-start
  7.2 3.7 copy-start.6
  7.2 3.7 copy-start.10
  9.5 1.3 copy-start.3
  19.3 24.6 %all-to-all-start = ((bf16[8,2,20480]{2,1,0:T(2,128)(2,1)}), bf16[8,2,20480]{2,1,0:T(2,128)(2,1)S(1)}, u32[]{:S(2)}, u32[]{:S(2)}) async-start(bf16[8,2,20480]{2,1,0:T(2,128)(2,1)} %reshape.330), calls=%async_computation | async-start | bytes 1310720 | tf_op jit(solution)/shard_map/all_to_all | solution.py:72
  48.0 35.2 %all-to-all-start.1 = ((f32[8,64,640]{2,1,0:T(8,128)}), f32[8,64,640]{2,1,0:T(8,128)S(1)}, u32[]{:S(2)}, u32[]{:S(2)}) async-start(f32[8,64,640]{2,1,0:T(8,128)} %copy.132), calls=%async_computation.1 | async-start | bytes 2621440 | tf_op jit(solution)/shard_map/all_to_all | solution.py:81
  83.2 35.2 %all-to-all-start.2 = ((f32[8,64,640]{2,1,0:T(8,128)}), f32[8,64,640]{2,1,0:T(8,128)S(1)}, u32[]{:S(2)}, u32[]{:S(2)}) async-start(f32[8,64,640]{2,1,0:T(8,128)} %copy.134), calls=%async_computation.2 | async-start | bytes 2621440 | tf_op jit(solution)/shard_map/all_to_all | solution.py:82
  118.4 1.6 copy-start.2
  174.2 41.1 %all-to-all-start.4 = ((f32[8,1,64,768]{3,2,1,0:T(8,128)}), f32[8,1,64,768]{3,2,1,0:T(8,128)S(1)}, u32[]{:S(2)}, u32[]{:S(2)}) async-start(f32[8,1,64,768]{3,2,1,0:T(8,128)} %fusion.48), calls=%async_computation.4 | async-start | bytes 3145728 | tf_op jit(solution)/shard_map/all_to_all | solution.py:99
  215.3 40.8 %all-to-all-start.3 = ((f32[1,512,768]{2,0,1:T(1,128)}), f32[1,512,768]{2,0,1:T(1,128)S(1)}, u32[]{:S(2)}, u32[]{:S(2)}) async-start(f32[1,512,768]{2,0,1:T(1,128)} %copy.154), calls=%async_computation.3 | async-start | bytes 3145728 | tf_op jit(solution)/shard_map/all_to_all | solution.py:97
  218.9 164.3 %all-reduce.5.cloned.1.call-start = ((), (), s32[]{:S(2)}) async-start(), calls=%async_computation.6 | async-start | bytes 2097152
  222.6 33.7 %copy-start.1 = (f32[8,64,768]{2,0,1:T(8,128)S(1)}, f32[8,64,768]{2,0,1:T(8,128)}, u32[]{:S(2)}) copy-start(f32[8,64,768]{2,0,1:T(8,128)} %fusion) | copy-start | bytes 4718596
  300.7 2.3 copy-start.4
  301.7 2.6 copy-start.5
  303.0 1.6 copy-start.7
  304.7 1.4 copy-start.11
  304.7 80.1 %copy-start.8 = (bf16[256,256]{1,0:T(8,128)(2,1)S(1)}, bf16[256,256]{1,0:T(8,128)(2,1)}, u32[]{:S(2)}) copy-start(bf16[256,256]{1,0:T(8,128)(2,1)} %param.7) | copy-start | bytes 393220
  306.1 79.1 %copy-start.9 = (bf16[256,256]{1,0:T(8,128)(2,1)S(1)}, bf16[256,256]{1,0:T(8,128)(2,1)}, u32[]{:S(2)}) copy-start(bf16[256,256]{1,0:T(8,128)(2,1)} %param.8) | copy-start | bytes 393220
  306.1 98.9 %all-reduce.7.cloned.1.call-start = ((), (), s32[]{:S(2)}) async-start(), calls=%async_computation.7 | async-start | bytes 1310720 | tf_op jit(solution)/shard_map/psum | solution.py:179
Sparse Core Ops, SparseCore 0:
  306.2 77.0 all-reduce.4
  386.3 18.5 all-reduce.6
